TPU v7x, 256 devices: a whole 4x4x8 slice. The times are simulated.
256 devices in a mesh: view: 16 (over x_lo, z), seq: 16 (over y, x_hi, core).
Axes of the slice: x: 4 (x_hi: 2, x_lo: 2; x = x_hi * 2 + x_lo), y: 4, z: 8, core: 2. Of those that a mesh axis runs over, the one named last changes fastest.
Arguments:
- tokens: bfloat16 [16, 6144, 1024], P('view', 'seq'), may hold values from -6 to 6
- w_cross_qkv: bfloat16 [1024, 3072], replicated, may hold values from -8 to 8
- w_cross_out: bfloat16 [1024, 1024], replicated, may hold values from -3 to 3
- w_temporal_qkv: bfloat16 [1024, 3072], P('view'), may hold values from -8 to 8
- w_temporal_out: bfloat16 [1024, 1024], P('view'), may hold values from -0.359375 to 0.359375
Outputs:
- cross_update: bfloat16 [16, 6144, 1024], P('view', 'seq')
- temporal_update: bfloat16 [16, 6144, 1024], P('view', 'seq')
All inputs are finite; a program needn't handle non-finite values.
Results may differ from a plain program's by a relative error of at most 0.02.
Values may be sent and summed in bfloat16 or wider, within the bound.
No kernel may reach another device: no remote copies, remote signals or barrier semaphores. Data moves between devices by JAX's collectives and lax.ppermute only.
A program may use at most 128 MiB of HBM per device.

v0:
```python
import jax
import jax.numpy as jnp
from jax import lax
from jax.sharding import PartitionSpec as P

HEADS = 16


def partner_2(shard, axis, distance):
    return lax.ppermute(shard, axis, [(i, i ^ 1 << distance) for i in range(lax.axis_size(axis))])


def shifted(value, axis, steps):
    count = lax.axis_size(axis)
    pairs = [(source, (source + steps) % count) for source in range(count)]
    return lax.ppermute(value, axis, pairs)


def layer_norm(inputs):
    widened = inputs.astype(jnp.float32)
    average = jnp.mean(widened, axis=-1, keepdims=True)
    centred = widened - average
    variance = jnp.mean(centred * centred, axis=-1, keepdims=True)
    return (centred * lax.rsqrt(variance + 1e-06)).astype(jnp.bfloat16)


def grouped_attention(queries, keys_all, values_all, groups):
    row_count, head_count, head_size = queries.shape
    per_group = head_count // groups
    score_scale = head_size ** (-0.5)

    def split_groups(source):
        return jnp.transpose(
            source.reshape(source.shape[0], groups, per_group, head_size), (1, 0, 2, 3)
        )

    def attend_group(members):
        group_query, group_keys, group_values = members
        scores = (
            jnp.einsum("tha,sha->hts", group_query, group_keys, preferred_element_type=jnp.float32)
            * score_scale
        )
        row_peak = jnp.max(scores, axis=-1, keepdims=True)
        weights = jnp.exp(scores - row_peak)
        totals = jnp.sum(weights, axis=-1)
        result = jnp.einsum(
            "hts,sha->tha",
            weights.astype(jnp.bfloat16),
            group_values,
            preferred_element_type=jnp.float32,
        )
        return (result / jnp.transpose(totals)[:, :, None]).astype(jnp.bfloat16)

    results = lax.map(
        attend_group, (split_groups(queries), split_groups(keys_all), split_groups(values_all))
    )
    return jnp.transpose(results, (1, 0, 2, 3)).reshape(row_count, head_count * head_size)


def temporal_attend(queries, keys_all, values_all):
    score_scale = queries.shape[-1] ** (-0.5)
    scores = (
        jnp.einsum("fsha,gsha->shfg", queries, keys_all, preferred_element_type=jnp.float32)
        * score_scale
    )
    row_peak = jnp.max(scores, axis=-1, keepdims=True)
    weights = jnp.exp(scores - row_peak)
    totals = jnp.sum(weights, axis=-1)
    result = jnp.einsum(
        "shfg,gsha->fsha",
        weights.astype(jnp.bfloat16),
        values_all,
        preferred_element_type=jnp.float32,
    )
    return (result / jnp.transpose(totals, (2, 0, 1))[..., None]).astype(jnp.bfloat16)


def per_device(tokens, w_cross_qkv, w_cross_out, w_temporal_qkv, w_temporal_out):
    own_rows = tokens[0]
    row_count, features = own_rows.shape
    head_size = features // HEADS
    normed = layer_norm(own_rows)
    projected = jnp.dot(normed, w_cross_qkv, preferred_element_type=jnp.float32).astype(
        jnp.bfloat16
    )
    queries = projected[:, :features]
    key_value = projected[:, features:]
    partner = partner_2(key_value, "seq", 0)
    whole_frame = jnp.concatenate([key_value, partner], 0)
    before = shifted(whole_frame, "view", 1)
    following = shifted(whole_frame, "view", -1)
    remote = jnp.concatenate([partner, before, following], 0)
    key_pairs = jnp.concatenate([key_value, remote], 0)
    attended = grouped_attention(
        queries.reshape(row_count, HEADS, head_size),
        key_pairs[:, :features].reshape(-1, HEADS, head_size),
        key_pairs[:, features:].reshape(-1, HEADS, head_size),
        4,
    )
    cross_rows = jnp.dot(attended, w_cross_out, preferred_element_type=jnp.float32).astype(
        jnp.bfloat16
    )
    residual = own_rows.astype(jnp.float32) + cross_rows.astype(jnp.float32)
    normed_two = layer_norm(residual)
    columns = normed_two
    temporal = jnp.dot(
        columns,
        lax.all_gather(w_temporal_qkv, "view", axis=0, tiled=True),
        preferred_element_type=jnp.float32,
    ).astype(jnp.bfloat16)
    spread = lax.all_to_all(
        temporal.reshape(row_count, 3, features), "seq", split_axis=2, concat_axis=0, tiled=True
    )
    frames = spread.shape[0] // (2 * row_count)
    group_heads = spread.shape[2] // head_size
    blocks = spread.reshape(frames, 2 * row_count, 3, group_heads, head_size)
    mixed_heads = temporal_attend(blocks[:, :, 0], blocks[:, :, 1], blocks[:, :, 2])
    mixed_heads = mixed_heads.reshape(spread.shape[0], group_heads * head_size)
    mixed_rows = lax.all_to_all(mixed_heads, "seq", split_axis=0, concat_axis=1, tiled=True)
    columns = mixed_rows
    temporal_rows = jnp.dot(
        columns,
        lax.all_gather(w_temporal_out, "view", axis=0, tiled=True),
        preferred_element_type=jnp.float32,
    ).astype(jnp.bfloat16)
    return (cross_rows[None], temporal_rows[None])


def solution(mesh):
    placed = (P("view", "seq", None), P(), P(), P("view", None), P("view", None))
    return jax.shard_map(
        per_device,
        mesh=mesh,
        in_specs=placed,
        out_specs=(P("view", "seq", None), P("view", "seq", None)),
        check_vma=False,
    )
```

profile of v0, /device:TPU:1, one launch (start us, length us, event | category | flops | bytes accessed | tf_op | source)
XLA Modules:
  0.0 429.0 jit_solution(2347345283628091648)
XLA Ops:
  10.2 5.8 %convolution_convert_fusion.1 = bf16[384,3072]{1,0:T(8,128)(2,1)S(1)} fusion(bf16[1024,3072]{1,0:T(8,128)(2,1)} %param.8, bf16[1,384,1024]{2,1,0:T(8,128)(2,1)} %param.7, f32[384]{0:T(512)S(1)} %add_rsqrt_fusion.1, f32[384]{0:T(512)S(1)} %broadcast_multiply_fusion.1), kind=kOutput, calls=%fused_computation.22 | convolution fusion | flops 2418671616 | bytes 9440256 | tf_op jit(solution)/shard_map/dot_general | solution.py:83
  32.1 119.6 %collective-permute-done.1 = bf16[768,2048]{1,0:T(8,128)(2,1)} collective-permute-done((bf16[768,2048]{1,0:T(8,128)(2,1)}, bf16[768,2048]{1,0:T(8,128)(2,1)}, u32[]{:S(2)}, u32[]{:S(2)}) %collective-permute-start.1) | collective-permute-done | bytes 3145760 | tf_op jit(solution)/shard_map/ppermute | solution.py:16
  154.9 7.7 %pad_maximum_fusion = bf16[2304,2048]{1,0:T(8,128)(2,1)} fusion(bf16[768,2048]{1,0:T(8,128)(2,1)} %collective-permute-done.2, bf16[768,2048]{1,0:T(8,128)(2,1)} %collective-permute-done.1, bf16[384,2048]{1,0:T(8,128)(2,1)} %copy-done.3, bf16[384,2048]{1,0:T(8,128)(2,1)} %copy-done.1), kind=kLoop, calls=%fused_computation.20 | loop fusion | flops 37748736 | bytes 18874368 | tf_op jit(solution)/shard_map/concatenate | solution.py:93
  162.6 8.6 %fusion.62 = (bf16[2304,1024]{1,0:T(8,128)(2,1)}, bf16[2304,1024]{1,0:T(8,128)(2,1)}) fusion(bf16[2304,2048]{1,0:T(8,128)(2,1)} %pad_maximum_fusion), kind=kLoop, calls=%fused_computation.60 | loop fusion | bytes 18874368 | tf_op jit(solution)/shard_map/slice | solution.py:96
  171.2 6.7 %copy.24 = bf16[2304,1024]{0,1:T(8,128)(2,1)} copy(bf16[2304,1024]{1,0:T(8,128)(2,1)} %get-tuple-element.42) | data formatting | bytes 9437184 | tf_op jit(solution)/shard_map/slice | solution.py:96
  177.9 6.7 %copy.22 = bf16[2304,1024]{0,1:T(8,128)(2,1)} copy(bf16[2304,1024]{1,0:T(8,128)(2,1)} %get-tuple-element.43) | data formatting | bytes 9437184 | tf_op jit(solution)/shard_map/slice | solution.py:97
  184.7 98.7 %while.10 = (s32[]{:T(128)}, bf16[4,384,4,64]{1,3,2,0:T(8,128)(2,1)}, bf16[4,2304,4,64]{1,3,2,0:T(8,128)(2,1)}, bf16[4,384,4,64]{1,3,2,0:T(8,128)(2,1)}, bf16[4,2304,4,64]{1,3,2,0:T(8,128)(2,1)}, /*index=5*/s32[]{:T(128)}) while((s32[]{:T(128)}, bf16[4,384,4,64]{1,3,2,0:T(8,128)(2,1)}, bf16[4,2304,4,64]{1,3,2,0:T(8,128)(2,1)}, ...), condition=%wide.region_5.6_spmd, body=%wide.region_2.5_spmd.sunk | while | flops 934474752 | bytes 45252676 | solution.py:54
  184.7 8.5 %multiply_reduce_fusion.4 = (f32[4,384]{1,0:T(4,128)S(1)}, f32[4,384,2304]{2,1,0:T(8,128)}) fusion(bf16[4,2304,4,64]{1,3,2,0:T(8,128)(2,1)} %get-tuple-element.102, s32[]{:T(128)} %get-tuple-element.92, bf16[4,384,4,64]{1,3,2,0:T(8,128)(2,1)} %get-tuple-element.101), kind=kOutput, calls=%fused_computation.1.clone.1 | convolution fusion | flops 460061184 | bytes 15539200 | tf_op jit(solution)/shard_map/while/body/eval_jaxpr/tha,sha->hts/dot_general | solution.py:40
  193.2 7.5 %fusion.76 = f32[4,384]{1,0:T(4,128)S(1)} fusion(f32[4,384,2304]{2,1,0:T(8,128)} %get-tuple-element.84, f32[4,384]{1,0:T(4,128)S(1)} %get-tuple-element.85), kind=kLoop, calls=%fused_computation.2.clone.1 | loop fusion | flops 10615296 | bytes 14168064 | tf_op jit(solution)/shard_map/while/body/eval_jaxpr/reduce_sum | solution.py:45
  200.7 8.7 %fusion.77 = bf16[4,384,4,64]{1,3,2,0:T(8,128)(2,1)} fusion(bf16[4,384,4,64]{1,3,2,0:T(8,128)(2,1)} %get-tuple-element.93, s32[]{:T(128)} %get-tuple-element.92, f32[4,384,2304]{2,1,0:T(8,128)} %get-tuple-element.84, f32[4,384]{1,0:T(4,128)S(1)} %get-tuple-element.85, bf16[4,2304,4,64]{1,3,2,0:T(8,128)(2,1)} %get-tuple-element.100, ...), kind=kOutput, calls=%fused_computation.14.clone.1 | convolution fusion | flops 463798272 | bytes 15545344 | tf_op jit(solution)/shard_map/while/body/eval_jaxpr/hts,sha->tha/dot_general | solution.py:46
  209.4 8.5 %multiply_reduce_fusion.4 = (f32[4,384]{1,0:T(4,128)S(1)}, f32[4,384,2304]{2,1,0:T(8,128)}) fusion(bf16[4,2304,4,64]{1,3,2,0:T(8,128)(2,1)} %get-tuple-element.102, s32[]{:T(128)} %get-tuple-element.92, bf16[4,384,4,64]{1,3,2,0:T(8,128)(2,1)} %get-tuple-element.101), kind=kOutput, calls=%fused_computation.1.clone.1 | convolution fusion | flops 460061184 | bytes 15539200 | tf_op jit(solution)/shard_map/while/body/eval_jaxpr/tha,sha->hts/dot_general | solution.py:40
  217.9 7.5 %fusion.76 = f32[4,384]{1,0:T(4,128)S(1)} fusion(f32[4,384,2304]{2,1,0:T(8,128)} %get-tuple-element.84, f32[4,384]{1,0:T(4,128)S(1)} %get-tuple-element.85), kind=kLoop, calls=%fused_computation.2.clone.1 | loop fusion | flops 10615296 | bytes 14168064 | tf_op jit(solution)/shard_map/while/body/eval_jaxpr/reduce_sum | solution.py:45
  225.3 8.7 %fusion.77 = bf16[4,384,4,64]{1,3,2,0:T(8,128)(2,1)} fusion(bf16[4,384,4,64]{1,3,2,0:T(8,128)(2,1)} %get-tuple-element.93, s32[]{:T(128)} %get-tuple-element.92, f32[4,384,2304]{2,1,0:T(8,128)} %get-tuple-element.84, f32[4,384]{1,0:T(4,128)S(1)} %get-tuple-element.85, bf16[4,2304,4,64]{1,3,2,0:T(8,128)(2,1)} %get-tuple-element.100, ...), kind=kOutput, calls=%fused_computation.14.clone.1 | convolution fusion | flops 463798272 | bytes 15545344 | tf_op jit(solution)/shard_map/while/body/eval_jaxpr/hts,sha->tha/dot_general | solution.py:46
  234.0 8.5 %multiply_reduce_fusion.4 = (f32[4,384]{1,0:T(4,128)S(1)}, f32[4,384,2304]{2,1,0:T(8,128)}) fusion(bf16[4,2304,4,64]{1,3,2,0:T(8,128)(2,1)} %get-tuple-element.102, s32[]{:T(128)} %get-tuple-element.92, bf16[4,384,4,64]{1,3,2,0:T(8,128)(2,1)} %get-tuple-element.101), kind=kOutput, calls=%fused_computation.1.clone.1 | convolution fusion | flops 460061184 | bytes 15539200 | tf_op jit(solution)/shard_map/while/body/eval_jaxpr/tha,sha->hts/dot_general | solution.py:40
  242.5 7.5 %fusion.76 = f32[4,384]{1,0:T(4,128)S(1)} fusion(f32[4,384,2304]{2,1,0:T(8,128)} %get-tuple-element.84, f32[4,384]{1,0:T(4,128)S(1)} %get-tuple-element.85), kind=kLoop, calls=%fused_computation.2.clone.1 | loop fusion | flops 10615296 | bytes 14168064 | tf_op jit(solution)/shard_map/while/body/eval_jaxpr/reduce_sum | solution.py:45
  250.0 8.7 %fusion.77 = bf16[4,384,4,64]{1,3,2,0:T(8,128)(2,1)} fusion(bf16[4,384,4,64]{1,3,2,0:T(8,128)(2,1)} %get-tuple-element.93, s32[]{:T(128)} %get-tuple-element.92, f32[4,384,2304]{2,1,0:T(8,128)} %get-tuple-element.84, f32[4,384]{1,0:T(4,128)S(1)} %get-tuple-element.85, bf16[4,2304,4,64]{1,3,2,0:T(8,128)(2,1)} %get-tuple-element.100, ...), kind=kOutput, calls=%fused_computation.14.clone.1 | convolution fusion | flops 463798272 | bytes 15545344 | tf_op jit(solution)/shard_map/while/body/eval_jaxpr/hts,sha->tha/dot_general | solution.py:46
  258.7 8.5 %multiply_reduce_fusion.4 = (f32[4,384]{1,0:T(4,128)S(1)}, f32[4,384,2304]{2,1,0:T(8,128)}) fusion(bf16[4,2304,4,64]{1,3,2,0:T(8,128)(2,1)} %get-tuple-element.102, s32[]{:T(128)} %get-tuple-element.92, bf16[4,384,4,64]{1,3,2,0:T(8,128)(2,1)} %get-tuple-element.101), kind=kOutput, calls=%fused_computation.1.clone.1 | convolution fusion | flops 460061184 | bytes 15539200 | tf_op jit(solution)/shard_map/while/body/eval_jaxpr/tha,sha->hts/dot_general | solution.py:40
  267.2 7.5 %fusion.76 = f32[4,384]{1,0:T(4,128)S(1)} fusion(f32[4,384,2304]{2,1,0:T(8,128)} %get-tuple-element.84, f32[4,384]{1,0:T(4,128)S(1)} %get-tuple-element.85), kind=kLoop, calls=%fused_computation.2.clone.1 | loop fusion | flops 10615296 | bytes 14168064 | tf_op jit(solution)/shard_map/while/body/eval_jaxpr/reduce_sum | solution.py:45
  274.6 8.7 %fusion.77 = bf16[4,384,4,64]{1,3,2,0:T(8,128)(2,1)} fusion(bf16[4,384,4,64]{1,3,2,0:T(8,128)(2,1)} %get-tuple-element.93, s32[]{:T(128)} %get-tuple-element.92, f32[4,384,2304]{2,1,0:T(8,128)} %get-tuple-element.84, f32[4,384]{1,0:T(4,128)S(1)} %get-tuple-element.85, bf16[4,2304,4,64]{1,3,2,0:T(8,128)(2,1)} %get-tuple-element.100, ...), kind=kOutput, calls=%fused_computation.14.clone.1 | convolution fusion | flops 463798272 | bytes 15545344 | tf_op jit(solution)/shard_map/while/body/eval_jaxpr/hts,sha->tha/dot_general | solution.py:46
  286.9 7.2 %convolution_convert_fusion = bf16[384,3072]{1,0:T(8,128)(2,1)} fusion(bf16[1024,3072]{1,0:T(8,128)(2,1)} %all-gather.3.cloned.1.call-done, bf16[384,1024]{1,0:T(8,128)(2,1)} %copy-done.5, bf16[1,384,1024]{2,1,0:T(8,128)(2,1)S(1)} %copy-done.2, f32[384]{0:T(512)S(1)} %add_rsqrt_fusion, f32[384]{0:T(512)S(1)} %broadcast_multiply_fusion), kind=kOutput, calls=%fused_computation.21 | convolution fusion | flops 2419458048 | bytes 10226688 | tf_op jit(solution)/shard_map/dot_general | solution.py:106
  298.3 5.3 %copy.26 = bf16[384,3,1024]{0,1,2:T(4,128)(2,1)} copy(bf16[384,3,1024]{0,2,1:T(8,128)(2,1)} %bitcast.134) | data formatting | bytes 4718592 | tf_op jit(solution)/shard_map/reshape | solution.py:112
  303.7 9.3 %all-to-all-start = ((bf16[384,3,1024]{0,1,2:T(4,128)(2,1)}), bf16[384,3,1024]{0,1,2:T(4,128)(2,1)}, u32[]{:S(2)}, u32[]{:S(2)}) async-start(bf16[384,3,1024]{0,1,2:T(4,128)(2,1)} %copy.26), calls=%async_computation | async-start | bytes 6291456 | tf_op jit(solution)/shard_map/all_to_all | solution.py:111
  313.7 52.2 %all-to-all-done = bf16[384,3,1024]{0,1,2:T(4,128)(2,1)} async-done(((bf16[384,3,1024]{0,1,2:T(4,128)(2,1)}), bf16[384,3,1024]{0,1,2:T(4,128)(2,1)}, u32[]{:S(2)}, u32[]{:S(2)}) %all-to-all-start) | async-done | bytes 2359328 | tf_op jit(solution)/shard_map/all_to_all | solution.py:111
  404.3 14.4 %all-to-all-done.1 = bf16[16,384,64]{1,2,0:T(8,128)(2,1)S(1)} async-done(((bf16[16,384,64]{1,2,0:T(8,128)(2,1)}), bf16[16,384,64]{1,2,0:T(8,128)(2,1)S(1)}, u32[]{:S(2)}, u32[]{:S(2)}) %all-to-all-start.1) | async-done | bytes 786464 | tf_op jit(solution)/shard_map/all_to_all | solution.py:119
  (55 shorter events, 72.6 us)
Async XLA Ops:
  7.2 276.2 %copy-start = (bf16[1024,1024]{1,0:T(8,128)(2,1)S(1)}, bf16[1024,1024]{1,0:T(8,128)(2,1)}, u32[]{:S(2)}) copy-start(bf16[1024,1024]{1,0:T(8,128)(2,1)} %param.9) | copy-start | bytes 6291460
  7.2 279.7 %all-gather.3.cloned.1.call-start = ((), (), s32[]{:S(2)}) async-start(), calls=%async_computation.2 | async-start | bytes 6684672 | tf_op jit(solution)/shard_map/all_gather | solution.py:108
  15.9 1.4 copy-start.4
  17.4 8.5 %copy-start.1 = (bf16[384,2048]{1,0:T(8,128)(2,1)}, bf16[384,2048]{1,0:T(8,128)(2,1)S(1)}, u32[]{:S(2)}) copy-start(bf16[384,2048]{1,0:T(8,128)(2,1)S(1)} %slice.28) | copy-start | bytes 4718596
  17.4 6.3 %collective-permute-start = (bf16[384,2048]{1,0:T(8,128)(2,1)S(1)}, bf16[384,2048]{1,0:T(8,128)(2,1)S(1)}, u32[]{:S(2)}, u32[]{:S(2)}) collective-permute-start(bf16[384,2048]{1,0:T(8,128)(2,1)S(1)} %slice.28), channel_id=1, source_target_pairs={{0,1},{1,0},{2,3},{3,2},{4,5},{5,4},{6,7},{7,6},{8,9},{9,8},{10,11... | collective-permute-start | bytes 4718600 | tf_op jit(solution)/shard_map/ppermute | solution.py:10
  20.6 10.3 %slice-start = ((bf16[384,3072]{1,0:T(8,128)(2,1)}), bf16[384,1024]{1,0:T(8,128)(2,1)S(1)}, s32[]{:S(2)}) async-start(bf16[384,3072]{1,0:T(8,128)(2,1)} %copy-done.4), calls=%async_computation.4 | async-start | bytes 1572864 | tf_op jit(solution)/shard_map/slice | solution.py:86
  23.7 2.2 copy-start.3
  25.9 125.9 %collective-permute-start.1 = (bf16[768,2048]{1,0:T(8,128)(2,1)}, bf16[768,2048]{1,0:T(8,128)(2,1)}, u32[]{:S(2)}, u32[]{:S(2)}) collective-permute-start(bf16[768,2048]{1,0:T(8,128)(2,1)} %pad_maximum_fusion.1), channel_id=1, source_target_pairs={{0,16},{16,32},{32,48},{48,64},{64,80},{80,96},{96,112},{112,128},... | collective-permute-start | bytes 9437192 | tf_op jit(solution)/shard_map/ppermute | solution.py:16
  25.9 129.0 %collective-permute-start.2 = (bf16[768,2048]{1,0:T(8,128)(2,1)}, bf16[768,2048]{1,0:T(8,128)(2,1)}, u32[]{:S(2)}, u32[]{:S(2)}) collective-permute-start(bf16[768,2048]{1,0:T(8,128)(2,1)} %pad_maximum_fusion.1), channel_id=1, source_target_pairs={{0,240},{16,0},{32,16},{48,32},{64,48},{80,64},{96,80},{112,96},{1... | collective-permute-start | bytes 9437192 | tf_op jit(solution)/shard_map/ppermute | solution.py:16
  184.7 98.7 %copy-start.2 = (bf16[1,384,1024]{2,1,0:T(8,128)(2,1)S(1)}, bf16[1,384,1024]{2,1,0:T(8,128)(2,1)}, u32[]{:S(2)}) copy-start(bf16[1,384,1024]{2,1,0:T(8,128)(2,1)} %param.7) | copy-start | bytes 2359300
  285.6 0.9 copy-start.5
  303.7 62.2 %all-to-all-start = ((bf16[384,3,1024]{0,1,2:T(4,128)(2,1)}), bf16[384,3,1024]{0,1,2:T(4,128)(2,1)}, u32[]{:S(2)}, u32[]{:S(2)}) async-start(bf16[384,3,1024]{0,1,2:T(4,128)(2,1)} %copy.26), calls=%async_computation | async-start | bytes 6291456 | tf_op jit(solution)/shard_map/all_to_all | solution.py:111
  313.0 91.3 %all-gather.5.cloned.1.call-start = ((), (), s32[]{:S(2)}) async-start(), calls=%async_computation.3 | async-start | bytes 2228224 | tf_op jit(solution)/shard_map/all_gather | solution.py:123
  390.1 1.4 copy-start.6
  399.7 19.0 %all-to-all-start.1 = ((bf16[16,384,64]{1,2,0:T(8,128)(2,1)}), bf16[16,384,64]{1,2,0:T(8,128)(2,1)S(1)}, u32[]{:S(2)}, u32[]{:S(2)}) async-start(bf16[16,384,64]{1,2,0:T(8,128)(2,1)} %copy.34), calls=%async_computation.1 | async-start | bytes 1572864 | tf_op jit(solution)/shard_map/all_to_all | solution.py:119
Sparse Core Ops, SparseCore 0:
  31.0 132.6 all-gather.2
  315.6 62.6 all-gather.4
where the time goes:
time: 430 us; the launch traced here: 429 us
  waiting for transfers between devices  193 us (45%)
  matrix products  93.3 us (22%)
  local copies, waits for them, and re-layouts  61.7 us (14%)
  other arithmetic  44.4 us (10%)
  starting transfers between devices  22.2 us (5%)
  between operations  14.2 us (3%)
    ppermute x2, waiting for transfers between devices, shifted(): return lax.ppermute(value, axis, pairs)  123 us
    all_to_all x1, waiting for transfers between devices, per_device(): lax.all_to_all(temporal.reshape(row_count, 3, features), 'seq', split_axi...  52.2 us
    dot_general x4, matrix products, attend_group(): jnp.einsum('hts,sha->tha', weights.astype(jnp.bfloat16), group_values, pr...  34.8 us
    dot_general x4, matrix products, attend_group(): jnp.einsum('tha,sha->hts', group_query, group_keys, preferred_element_typ...  34 us
    reduce_sum x4, other arithmetic, attend_group(): totals = jnp.sum(weights, axis=-1)  29.8 us
    slice x2, local copies, waits for them, and re-layouts, per_device(): key_pairs[:, :features].reshape(-1, HEADS, head_size)  15.3 us
    all_to_all x1, waiting for transfers between devices, per_device(): lax.all_to_all(mixed_heads, 'seq', split_axis=0, concat_axis=1, tiled=True)  14.4 us
    unnamed x17, local copies, waits for them, and re-layouts  10.5 us
  transfers between devices with their start and end apart: 7, of which 5 were waited for; matrix products, arithmetic and copies ran while one was open for 38% of the time, Pallas kernels for 0%

commit v1 on v0

v1 whole, which is shorter than its diff:
```python
import functools

import jax
import jax.numpy as jnp
from jax import lax
from jax.experimental import pallas as pl
from jax.experimental.pallas import tpu as pltpu
from jax.sharding import Mesh
from jax.sharding import PartitionSpec as P

HEADS = 16
HD = 64
PAIR = 2 * HD
QUAD = 4 * HD
LOG2E = 1.4426950408889634
VMEM_LIMIT = 56 * 1024 * 1024
F32 = jnp.float32
BF16 = jnp.bfloat16


def dot(a, b):
    return jnp.dot(a, b, preferred_element_type=F32)


def layer_norm(rows):
    centred = rows - jnp.mean(rows, axis=-1, keepdims=True)
    variance = jnp.mean(centred * centred, axis=-1, keepdims=True)
    return (centred * lax.rsqrt(variance + 1e-06)).astype(BF16)


def lanes_of(width, index, rows=1):
    lane = lax.broadcasted_iota(jnp.int32, (rows, width), 1)
    return jnp.where(lane // HD == index, 1.0, 0.0).astype(BF16)


def cross_step_kernel(first, last, row_block, *refs):
    refs = list(refs)
    refs.pop(0)
    x_refs = [refs.pop(0), refs.pop(0)]
    if first:
        wq_ref = refs.pop(0)
    wk_ref, wv_ref = refs.pop(0), refs.pop(0)
    if not first:
        q_ref, o_in, m_in, l_in = (refs.pop(0) for _ in range(4))
    if first:
        q_ref = refs.pop(0)
    if last:
        halves = [refs.pop(0), refs.pop(0)]
    else:
        o_out, m_out, l_out = (refs.pop(0) for _ in range(3))
    norm_s, kt_s, v_s = refs
    half = x_refs[0].shape[0]
    keys = 2 * half
    pairs = kt_s.shape[0]
    step = pl.program_id(0)

    @pl.when(step == 0)
    def _():
        for part, x_ref in enumerate(x_refs):
            norm_s[part * half : (part + 1) * half, :] = layer_norm(x_ref[...].astype(F32))
        normed = norm_s[...]
        if first:
            queries = (dot(normed, wq_ref[...]) * (HD**-0.5 * LOG2E)).astype(BF16)
            for pair in range(pairs):
                q_ref[pair] = queries[:, pair * PAIR : (pair + 1) * PAIR]
        made_keys = dot(normed, wk_ref[...]).astype(BF16)
        made_values = dot(normed, wv_ref[...]).astype(BF16)
        for pair in range(pairs):
            kt_s[pair] = made_keys[:, pair * PAIR : (pair + 1) * PAIR].T
            v_s[pair, :, :PAIR] = made_values[:, pair * PAIR : (pair + 1) * PAIR]
            v_s[pair, :, PAIR:] = jnp.ones((keys, PAIR), BF16)

    index = step if first else 0
    transposed, values = kt_s[step], v_s[step]
    low = lax.broadcasted_iota(jnp.int32, (row_block, PAIR), 1) < HD
    for start in range(0, keys, row_block):
        rows = slice(start, start + row_block)
        queries = q_ref[index, rows, :]
        peaks, sums = [], []
        for head in range(2):
            scores = dot(queries * lanes_of(PAIR, head), transposed)
            peak = jnp.max(scores, axis=-1, keepdims=True)
            if not first:
                peak = jnp.maximum(peak, m_in[0, rows, head * HD : head * HD + 1])
            weights = jnp.exp2(scores - peak).astype(BF16)
            peaks.append(peak)
            sums.append(dot(weights, values))
        peak = jnp.where(low, peaks[0], peaks[1])
        result = jnp.where(low, sums[0][:, :PAIR], sums[1][:, :PAIR])
        total = jnp.where(low, sums[0][:, PAIR:], sums[1][:, PAIR:])
        if not first:
            scale = jnp.exp2(m_in[0, rows, :] - peak)
            result = result + scale * o_in[0, rows, :]
            total = total + scale * l_in[0, rows, :]
        if last:
            part, offset = divmod(start, half)
            halves[part][offset : offset + row_block, :] = (result / total).astype(BF16)
        else:
            o_out[0, rows, :] = result
            m_out[0, rows, :] = peak
            l_out[0, rows, :] = total


def cross_step(core, xs, w_cross_qkv, state=None, last=False, row_block=384):
    first = state is None
    half, features = xs[0].shape
    keys = 2 * half
    columns = features // 2
    pairs = columns // PAIR
    whole = pl.BlockSpec((half, features), lambda p, c: (0, 0))
    column = lambda which: pl.BlockSpec((features, columns), lambda p, c: (0, 2 * which + c[0]))
    by_pair = pl.BlockSpec((1, keys, PAIR), lambda p, c: (p, 0, 0))
    all_pairs = pl.BlockSpec((pairs, keys, PAIR), lambda p, c: (0, 0, 0))
    kept = jax.ShapeDtypeStruct((pairs, keys, PAIR), F32)
    in_specs = [whole, whole] + [column(which) for which in ((0, 1, 2) if first else (1, 2))]
    operands = list(xs) + [w_cross_qkv] * (3 if first else 2)
    out_specs, out_shape = [], []
    if first:
        out_specs.append(all_pairs)
        out_shape.append(jax.ShapeDtypeStruct((pairs, keys, PAIR), BF16))
    else:
        in_specs += [by_pair] * 4
        operands += list(state)
    if last:
        out_specs += [pl.BlockSpec((half, PAIR), lambda p, c: (0, p))] * 2
        out_shape += [jax.ShapeDtypeStruct((half, columns), BF16)] * 2
    else:
        out_specs += [by_pair] * 3
        out_shape += [kept] * 3
    flops = 2 * keys * features * columns * (3 if first else 2) + 16 * keys * keys * PAIR * pairs
    return pl.pallas_call(
        functools.partial(cross_step_kernel, first, last, row_block),
        grid_spec=pltpu.PrefetchScalarGridSpec(
            num_scalar_prefetch=1,
            grid=(pairs,),
            in_specs=in_specs,
            out_specs=out_specs,
            scratch_shapes=[
                pltpu.VMEM((keys, features), BF16),
                pltpu.VMEM((pairs, PAIR, keys), BF16),
                pltpu.VMEM((pairs, keys, 2 * PAIR), BF16),
            ],
        ),
        out_shape=out_shape,
        compiler_params=pltpu.CompilerParams(vmem_limit_bytes=VMEM_LIMIT),
        cost_estimate=pl.CostEstimate(
            flops=flops, bytes_accessed=12 * 2**20, transcendentals=2 * keys * keys * pairs
        ),
        name="cross_first" if first else "cross_last" if last else "cross_middle",
    )(core, *operands)


def cross_out_kernel(core_ref, mine_ref, other_ref, x_ref, wm_ref, wo_ref, cross_ref, norm_ref):
    made = dot(mine_ref[...], wm_ref[...]) + dot(other_ref[...], wo_ref[...])
    cross_ref[...] = made.astype(BF16)
    residual = x_ref[...].astype(F32) + cross_ref[...].astype(F32)
    norm_ref[...] = layer_norm(residual)


def cross_out(core, mine, other, tokens, w_cross_out):
    rows, features = tokens.shape
    whole = lambda shape: pl.BlockSpec(shape, lambda s, c: (0, 0))
    half = features // 2
    return pl.pallas_call(
        cross_out_kernel,
        grid_spec=pltpu.PrefetchScalarGridSpec(
            num_scalar_prefetch=1,
            grid=(1,),
            in_specs=[
                whole((rows, half)),
                whole((rows, half)),
                whole((rows, features)),
                pl.BlockSpec((half, features), lambda s, c: (c[0], 0)),
                pl.BlockSpec((half, features), lambda s, c: (1 - c[0], 0)),
            ],
            out_specs=[whole((rows, features))] * 2,
        ),
        out_shape=[jax.ShapeDtypeStruct((rows, features), BF16)] * 2,
        compiler_params=pltpu.CompilerParams(vmem_limit_bytes=VMEM_LIMIT),
        cost_estimate=pl.CostEstimate(
            flops=2 * rows * features * features, bytes_accessed=6 * 2**20, transcendentals=0
        ),
        name="cross_out",
    )(core, mine, other, tokens, w_cross_out, w_cross_out)


GROUP = 16


def temporal_kernel(core_ref, x_ref, *refs):
    mine_refs, other_refs = refs[:3], refs[3:6]
    wo_ref, out_ref, x_s, att_s, acc_s = refs[6:]
    frames, positions, _ = x_ref.shape
    groups = positions // GROUP
    size = frames * GROUP
    step = pl.program_id(0)

    @pl.when(step == 0)
    def _():
        for group in range(groups):
            for frame in range(frames):
                x_s[pl.ds(group * size + frame * GROUP, GROUP), :] = x_ref[
                    frame, group * GROUP : (group + 1) * GROUP, :
                ]

    def attend(w_refs):
        rows = x_s[...]
        queries = (dot(rows, w_refs[0][...]) * (HD**-0.5 * LOG2E)).astype(BF16)
        keys = dot(rows, w_refs[1][...]).astype(BF16)
        values = dot(rows, w_refs[2][...]).astype(BF16)
        row = lax.broadcasted_iota(jnp.int32, (size, size), 0)
        column = lax.broadcasted_iota(jnp.int32, (size, size), 1)
        same = row % GROUP == column % GROUP
        head_of = lax.broadcasted_iota(jnp.int32, (size, QUAD), 1) // HD
        for group in range(groups):
            part = slice(group * size, (group + 1) * size)
            transposed = keys[part].T
            attended = jnp.zeros((size, QUAD), F32)
            for head in range(QUAD // HD):
                scores = dot(queries[part] * lanes_of(QUAD, head), transposed)
                scores = jnp.where(same, scores, -jnp.inf)
                weights = jnp.exp2(scores - jnp.max(scores, axis=-1, keepdims=True))
                total = jnp.sum(weights, axis=-1, keepdims=True)
                result = dot(weights.astype(BF16), values[part]) / total
                attended = jnp.where(head_of == head, result, attended)
            att_s[part, :] = attended.astype(BF16)

    half_steps = pl.num_programs(0) // 2

    @pl.when(step < half_steps)
    def _():
        attend(mine_refs)

    @pl.when(step >= half_steps)
    def _():
        attend(other_refs)

    made = dot(att_s[...], wo_ref[...])

    @pl.when(step == 0)
    def _():
        acc_s[...] = made

    @pl.when(step > 0)
    def _():
        acc_s[...] += made

    @pl.when(step == pl.num_programs(0) - 1)
    def _():
        for group in range(groups):
            for frame in range(frames):
                out_ref[frame, group * GROUP : (group + 1) * GROUP, :] = acc_s[
                    pl.ds(group * size + frame * GROUP, GROUP), :
                ].astype(BF16)


def temporal(core, rows, mine, other, w_out):
    frames, positions, features = rows.shape
    count = frames * positions
    steps = features // QUAD
    whole = pl.BlockSpec((frames, positions, features), lambda j, c: (0, 0, 0))

    def column(which, own):
        def index(j, c):
            inside = jnp.minimum(j, 1) if own else jnp.maximum(j - 2, 0)
            return (0, 2 * which + inside)

        return pl.BlockSpec((features, QUAD), index)

    def out_rows(j, c):
        return (jnp.where(j < 2, 2 * c[0] + j, 2 * (1 - c[0]) + j - 2), 0)

    return pl.pallas_call(
        temporal_kernel,
        grid_spec=pltpu.PrefetchScalarGridSpec(
            num_scalar_prefetch=1,
            grid=(steps,),
            in_specs=[whole]
            + [column(which, True) for which in range(3)]
            + [column(which, False) for which in range(3)]
            + [pl.BlockSpec((QUAD, features), out_rows)],
            out_specs=whole,
            scratch_shapes=[
                pltpu.VMEM((count, features), BF16),
                pltpu.VMEM((count, QUAD), BF16),
                pltpu.VMEM((count, features), F32),
            ],
        ),
        out_shape=jax.ShapeDtypeStruct(rows.shape, BF16),
        compiler_params=pltpu.CompilerParams(vmem_limit_bytes=VMEM_LIMIT),
        cost_estimate=pl.CostEstimate(
            flops=8 * count * features * features, bytes_accessed=10 * 2**20, transcendentals=0
        ),
        name="temporal",
    )(core, rows, mine, mine, mine, other, other, other, w_out)


VIEW = ("xl", "z")
FRAME = ("y", "xh")
SWAP = [(0, 1), (1, 0)]


def per_device(tokens, w_cross_qkv, w_cross_out, w_temporal_qkv, w_temporal_out):
    own = tokens[0]
    rows, features = own.shape
    half = features // 2
    core_index = lax.axis_index("c")
    core = core_index.astype(jnp.int32).reshape(1)
    views = lax.axis_size(VIEW)
    forward = [(i, (i + 1) % views) for i in range(views)]
    backward = [(i, (i - 1) % views) for i in range(views)]

    partner = lax.ppermute(own, "c", SWAP)
    before = lax.ppermute(own, VIEW, forward)
    after = lax.ppermute(own, VIEW, backward)

    shard = w_temporal_qkv.reshape(-1, 3, 2, half)
    shard = lax.dynamic_index_in_dim(shard, core_index, 2, keepdims=False).reshape(-1, 3 * half)
    w_mine = lax.all_gather(shard, VIEW, axis=0, tiled=True)
    w_other = lax.ppermute(w_mine, "c", SWAP)
    w_out = lax.all_gather(w_temporal_out, VIEW, axis=0, tiled=True)

    state = cross_step(core, (own, partner), w_cross_qkv)
    before_other = lax.ppermute(before, "c", SWAP)
    after_other = lax.ppermute(after, "c", SWAP)
    state = (state[0],) + tuple(cross_step(core, (before, after), w_cross_qkv, state))
    mine, theirs = cross_step(core, (before_other, after_other), w_cross_qkv, state, last=True)
    other = lax.ppermute(theirs, "c", SWAP)
    cross_rows, normed = cross_out(core, mine, other, own, w_cross_out)

    frames = lax.axis_size(FRAME)
    spread = lax.all_to_all(normed, FRAME, split_axis=0, concat_axis=0, tiled=True)
    updated = temporal(
        core, spread.reshape(frames, rows // frames, features), w_mine, w_other, w_out
    )
    temporal_rows = lax.all_to_all(
        updated.reshape(rows, features), FRAME, split_axis=0, concat_axis=0, tiled=True
    )
    return (cross_rows[None], temporal_rows[None])


def solution(mesh):
    fine = Mesh(mesh.devices.reshape(2, 8, 4, 2, 2), ("xl", "z", "y", "xh", "c"))
    by_token = P(VIEW, FRAME + ("c",), None)
    placed = (by_token, P(), P(), P(VIEW, None), P(VIEW, None))
    return jax.shard_map(
        per_device,
        mesh=fine,
        in_specs=placed,
        out_specs=(by_token, by_token),
        check_vma=False,
    )
```

time: 430 us -> 211 us (0.49)
  waiting for transfers between devices: 193 us -> 65.6 us
  matrix products: 93.3 us -> 0 us
  Pallas kernels: 0 us -> 67.7 us
  local copies, waits for them, and re-layouts: 61.7 us -> 7.74 us
  other arithmetic: 44.4 us -> 0 us
  blocking collectives: 0 us -> 38.6 us
  starting transfers between devices: 22.2 us -> 16.9 us
    ppermute x3 -> x7, waiting for transfers between devices: 126 us -> 1.66 us  [the longest x1 1.65 us: per_device(): other = lax.ppermute(theirs, 'c', SWAP)]
    dot_general x14 -> x0, matrix products: 93.3 us -> none  [the longest x4 34.8 us: attend_group(): jnp.einsum('hts,sha->tha', weights.astype(jnp.bfloat16), group_values, pr...]
    pallas_call x0 -> x5, Pallas kernels: none -> 67.7 us  [the longest x3 47.8 us: cross_step(): pl.pallas_call(functools.partial(cross_step_kernel, first, last, row_bloc...]
    all_to_all x2 -> x0, waiting for transfers between devices: 66.6 us -> none  [the longest x1 52.2 us: per_device(): lax.all_to_all(temporal.reshape(row_count, 3, features), 'seq', split_axi...]
    all_gather x2, waiting for transfers between devices: 0.03 us -> 63.3 us  [the longest x1 63.3 us: per_device(): w_mine = lax.all_gather(shard, VIEW, axis=0, tiled=True)]
    all_to_all x0 -> x2, blocking collectives: none -> 38.6 us  [the longest x1 21.8 us: per_device(): lax.all_to_all(normed, FRAME, split_axis=0, concat_axis=0, tiled=True)]
    reduce_sum x8 -> x0, other arithmetic: 34.5 us -> none  [the longest x4 29.8 us: attend_group(): totals = jnp.sum(weights, axis=-1)]
    slice x8 -> x0, local copies, waits for them, and re-layouts: 26.3 us -> none  [the longest x2 15.3 us: per_device(): key_pairs[:, :features].reshape(-1, HEADS, head_size)]
  transfers between devices with their start and end apart: 7 -> 9, of which waited for: 5 -> 2; matrix products, arithmetic and copies ran while one was open for 38% -> 0% of each run, Pallas kernels for 0% -> 25%
where the time goes in v1:
time: 211 us
  Pallas kernels  67.7 us (32%)
  waiting for transfers between devices  65.6 us (31%)
  blocking collectives  38.6 us (18%)
  starting transfers between devices  16.9 us (8%)
  between operations  14.1 us (7%)
  local copies, waits for them, and re-layouts  7.74 us (4%)
    all_gather x1, waiting for transfers between devices, per_device(): w_mine = lax.all_gather(shard, VIEW, axis=0, tiled=True)  63.3 us
    pallas_call x3, Pallas kernels, cross_step(): pl.pallas_call(functools.partial(cross_step_kernel, first, last, row_bloc...  47.8 us
    all_to_all x1, blocking collectives, per_device(): lax.all_to_all(normed, FRAME, split_axis=0, concat_axis=0, tiled=True)  21.8 us
    all_to_all x1, blocking collectives, per_device(): lax.all_to_all(updated.reshape(rows, features), FRAME, split_axis=0, conc...  16.7 us
    pallas_call x1, Pallas kernels, temporal(): pl.pallas_call(temporal_kernel, grid_spec=pltpu.PrefetchScalarGridSpec(nu...  15.7 us
    ppermute x1, starting transfers between devices, per_device(): w_other = lax.ppermute(w_mine, 'c', SWAP)  7.55 us
    unnamed x10, local copies, waits for them, and re-layouts  5.17 us
    ppermute x1, starting transfers between devices, per_device(): after = lax.ppermute(own, VIEW, backward)  4.96 us
  transfers between devices with their start and end apart: 9, of which 2 were waited for; matrix products, arithmetic and copies ran while one was open for 0% of the time, Pallas kernels for 25%

profile of v1, /device:TPU:1, one launch (start us, length us, event | category | flops | bytes accessed | tf_op | source)
XLA Modules:
  0.0 210.7 jit_solution(4954861645544444238)
XLA Ops:
  7.2 1.3 reshape.24
  8.5 1.3 dynamic-slice_reduce_fusion
  9.8 0.7 copy.10
  10.6 0.7 all-gather.5.cloned.1.call-update
  11.3 2.5 %collective-permute-start = (bf16[384,1024]{1,0:T(8,128)(2,1)}, bf16[384,1024]{1,0:T(8,128)(2,1)}, u32[]{:S(2)}, u32[]{:S(2)}) collective-permute-start(bf16[384,1024]{1,0:T(8,128)(2,1)} %bitcast.1.refs_1_.x_ref), channel_id=1, source_target_pairs={{0,16},{16,32},{32,48},{48,64},{64,80},{80,96},{96,112},{112,128},... | collective-permute-start | bytes 2359304 | tf_op jit(solution)/shard_map/ppermute | solution.py:314
  13.8 5.0 %collective-permute-start.2 = (bf16[384,1024]{1,0:T(8,128)(2,1)}, bf16[384,1024]{1,0:T(8,128)(2,1)}, u32[]{:S(2)}, u32[]{:S(2)}) collective-permute-start(bf16[384,1024]{1,0:T(8,128)(2,1)} %bitcast.1.refs_1_.x_ref), channel_id=1, source_target_pairs={{0,240},{16,0},{32,16},{48,32},{64,48},{80,64},{96,80},{112,96},{1... | collective-permute-start | bytes 2359304 | tf_op jit(solution)/shard_map/ppermute | solution.py:315
  18.8 1.0 collective-permute-start.4
  19.8 63.3 %all-gather.3.cloned.1.call-done.refs_0_.refs_1_.refs_2_ = bf16[1024,1536]{1,0:T(8,128)(2,1)} async-done(((bf16[64,1536]{1,0:T(8,128)(2,1)}), bf16[1024,1536]{1,0:T(8,128)(2,1)}) %all-gather.3.cloned.1.call-update) | async-done | bytes 3145744 | tf_op jit(solution)/shard_map/all_gather | solution.py:319
  83.0 7.5 %collective-permute-start.6 = (bf16[1024,1536]{1,0:T(8,128)(2,1)}, bf16[1024,1536]{1,0:T(8,128)(2,1)S(1)}, u32[]{:S(2)}, u32[]{:S(2)}) collective-permute-start(bf16[1024,1536]{1,0:T(8,128)(2,1)} %all-gather.3.cloned.1.call-done.refs_0_.refs_1_.refs_2_), channel_id=1, source_target_pairs={{0,1},{1,0},{2,3},{3,2},{4,5},{5,4},{6,7},{7,6},{8,9},{9,8},{10,11... | collective-permute-start | bytes 9437192 | tf_op jit(solution)/shard_map/ppermute | solution.py:320
  90.6 0.5 collective-permute-start.3
  91.1 14.5 %cross_first.1 = (bf16[4,768,128]{2,1,0:T(8,128)(2,1)}, f32[4,768,128]{2,1,0:T(8,128)}, f32[4,768,128]{2,1,0:T(8,128)}, f32[4,768,128]{2,1,0:T(8,128)}) custom-call(s32[1]{0:T(128)} %bitcast.refs_0_.core_ref, bf16[384,1024]{1,0:T(8,128)(2,1)} %bitcast.1.refs_1_.x_ref, bf16[384,1024]{1,0:T(8,128)(2,1)} %collective-permute-done.4.refs_2_, ...), custom_call_target="tpu_custom_call" | custom-call | flops 7247757312 | bytes 12582912 | tf_op jit(solution)/shard_map/cross_first/pallas_call | solution.py:131
  105.6 16.7 %cross_middle.1 = (f32[4,768,128]{2,1,0:T(8,128)}, f32[4,768,128]{2,1,0:T(8,128)}, f32[4,768,128]{2,1,0:T(8,128)}) custom-call(s32[1]{0:T(128)} %bitcast.refs_0_.core_ref, bf16[384,1024]{1,0:T(8,128)(2,1)} %collective-permute-done.refs_1_, bf16[384,1024]{1,0:T(8,128)(2,1)} %collective-permute-done.2.refs_2_, bf16[1024,3072]{1,0:T(8,128)(2,1)} %refs_4_.5, ...), custom_call_target="tpu_custom_call" | custom-call | flops 6442450944 | bytes 12582912 | tf_op jit(solution)/shard_map/cross_middle/pallas_call | solution.py:131
  122.4 0.8 copy-done.2
  123.2 0.3 copy-done.3
  123.5 16.5 %cross_last.1 = (bf16[384,512]{1,0:T(8,128)(2,1)}, bf16[384,512]{1,0:T(8,128)(2,1)}) custom-call(s32[1]{0:T(128)} %bitcast.refs_0_.core_ref, bf16[384,1024]{1,0:T(8,128)(2,1)} %copy-done.2, bf16[384,1024]{1,0:T(8,128)(2,1)} %copy-done.3, bf16[1024,3072]{1,0:T(8,128)(2,1)} %refs_4_.5, bf16[1024,3072]{1,0:T(8,128)(2,1)} %refs_4_.5, ...), custom_call_target="tpu_custom_call" | custom-call | flops 6442450944 | bytes 12582912 | tf_op jit(solution)/shard_map/cross_last/pallas_call | solution.py:131
  140.0 0.3 collective-permute-start.5
  140.3 1.6 collective-permute-done.5.other_ref
  142.0 0.8 copy-done.1
  142.7 4.2 %cross_out.1 = (bf16[384,1024]{1,0:T(8,128)(2,1)}, bf16[384,1024]{1,0:T(8,128)(2,1)}) custom-call(s32[1]{0:T(128)} %bitcast.refs_0_.core_ref, bf16[384,512]{1,0:T(8,128)(2,1)} %get-tuple-element.20.mine_ref, bf16[384,512]{1,0:T(8,128)(2,1)} %copy-done.1, bf16[384,1024]{1,0:T(8,128)(2,1)} %bitcast.1.refs_1_.x_ref, bf16[1024,1024]{1,0:T(8,128)(2,1)} %wo_ref.1, ...), custom_call_target="tpu_custom_call" | custom-call | flops 805306368 | bytes 6291456 | tf_op jit(solution)/shard_map/cross_out/pallas_call | solution.py:164
  147.0 21.8 %all_to_all.15.x_ref = bf16[8,48,1024]{2,1,0:T(8,128)(2,1)} all-to-all(bf16[8,48,1024]{2,1,0:T(8,128)(2,1)} %bitcast.10), channel_id=1, replica_groups=mesh['xl'=2,'z'=8,'y'=4,'xh'=2,'c'=2] {'y','xh'}, dimensions={0} | all-to-all | bytes 1572864 | tf_op jit(solution)/shard_map/all_to_all | solution.py:332
  168.8 1.7 copy-done
  170.5 15.7 %temporal.1 = bf16[8,48,1024]{2,1,0:T(8,128)(2,1)} custom-call(s32[1]{0:T(128)} %bitcast.refs_0_.core_ref, bf16[8,48,1024]{2,1,0:T(8,128)(2,1)} %all_to_all.15.x_ref, bf16[1024,1536]{1,0:T(8,128)(2,1)} %all-gather.3.cloned.1.call-done.refs_0_.refs_1_.refs_2_, bf16[1024,1536]{1,0:T(8,128)(2,1)} %all-gather.3.cloned.1.call-done.refs_0_.refs_1_.refs_2_, ...), custom_call_target="tpu_custom_call" | custom-call | flops 3221225472 | bytes 10485760 | tf_op jit(solution)/shard_map/temporal/pallas_call | solution.py:273
  186.2 16.7 %all_to_all.16 = bf16[8,48,1024]{2,1,0:T(8,128)(2,1)S(1)} all-to-all(bf16[8,48,1024]{2,1,0:T(8,128)(2,1)} %temporal.1), channel_id=1, replica_groups=mesh['xl'=2,'z'=8,'y'=4,'xh'=2,'c'=2] {'y','xh'}, dimensions={0} | all-to-all | bytes 1572864 | tf_op jit(solution)/shard_map/all_to_all | solution.py:336
  202.9 0.9 copy.12
  (15 shorter events, 0.1 us)
Async XLA Ops:
  7.2 75.9 %all-gather.3.cloned.1.call-start = ((), (), s32[]{:S(2)}) async-start(), calls=%async_computation.2 | async-start | bytes 3342336 | tf_op jit(solution)/shard_map/all_gather | solution.py:319
  10.5 158.3 %all-gather.5.cloned.1.call-start = ((), (), s32[]{:S(2)}) async-start(), calls=%async_computation.3 | async-start | bytes 2228224 | tf_op jit(solution)/shard_map/all_gather | solution.py:321
  11.3 79.3 %collective-permute-start = (bf16[384,1024]{1,0:T(8,128)(2,1)}, bf16[384,1024]{1,0:T(8,128)(2,1)}, u32[]{:S(2)}, u32[]{:S(2)}) collective-permute-start(bf16[384,1024]{1,0:T(8,128)(2,1)} %bitcast.1.refs_1_.x_ref), channel_id=1, source_target_pairs={{0,16},{16,32},{32,48},{48,64},{64,80},{80,96},{96,112},{112,128},... | collective-permute-start | bytes 2359304 | tf_op jit(solution)/shard_map/ppermute | solution.py:314
  13.8 76.7 %collective-permute-start.2 = (bf16[384,1024]{1,0:T(8,128)(2,1)}, bf16[384,1024]{1,0:T(8,128)(2,1)}, u32[]{:S(2)}, u32[]{:S(2)}) collective-permute-start(bf16[384,1024]{1,0:T(8,128)(2,1)} %bitcast.1.refs_1_.x_ref), channel_id=1, source_target_pairs={{0,240},{16,0},{32,16},{48,32},{64,48},{80,64},{96,80},{112,96},{1... | collective-permute-start | bytes 2359304 | tf_op jit(solution)/shard_map/ppermute | solution.py:315
  18.8 72.3 %collective-permute-start.4 = (bf16[384,1024]{1,0:T(8,128)(2,1)}, bf16[384,1024]{1,0:T(8,128)(2,1)}, u32[]{:S(2)}, u32[]{:S(2)}) collective-permute-start(bf16[384,1024]{1,0:T(8,128)(2,1)} %bitcast.1.refs_1_.x_ref), channel_id=1, source_target_pairs={{0,1},{1,0},{2,3},{3,2},{4,5},{5,4},{6,7},{7,6},{8,9},{9,8},{10,11... | collective-permute-start | bytes 2359304 | tf_op jit(solution)/shard_map/ppermute | solution.py:313
  83.0 85.8 %collective-permute-start.6 = (bf16[1024,1536]{1,0:T(8,128)(2,1)}, bf16[1024,1536]{1,0:T(8,128)(2,1)S(1)}, u32[]{:S(2)}, u32[]{:S(2)}) collective-permute-start(bf16[1024,1536]{1,0:T(8,128)(2,1)} %all-gather.3.cloned.1.call-done.refs_0_.refs_1_.refs_2_), channel_id=1, source_target_pairs={{0,1},{1,0},{2,3},{3,2},{4,5},{5,4},{6,7},{7,6},{8,9},{9,8},{10,11... | collective-permute-start | bytes 9437192 | tf_op jit(solution)/shard_map/ppermute | solution.py:320
  90.6 31.8 %collective-permute-start.1 = (bf16[384,1024]{1,0:T(8,128)(2,1)}, bf16[384,1024]{1,0:T(8,128)(2,1)S(1)}, u32[]{:S(2)}, u32[]{:S(2)}) collective-permute-start(bf16[384,1024]{1,0:T(8,128)(2,1)} %collective-permute-done.refs_1_), channel_id=1, source_target_pairs={{0,1},{1,0},{2,3},{3,2},{4,5},{5,4},{6,7},{7,6},{8,9},{9,8},{10,11... | collective-permute-start | bytes 2359304 | tf_op jit(solution)/shard_map/ppermute | solution.py:324
  90.6 31.8 %collective-permute-start.3 = (bf16[384,1024]{1,0:T(8,128)(2,1)}, bf16[384,1024]{1,0:T(8,128)(2,1)S(1)}, u32[]{:S(2)}, u32[]{:S(2)}) collective-permute-start(bf16[384,1024]{1,0:T(8,128)(2,1)} %collective-permute-done.2.refs_2_), channel_id=1, source_target_pairs={{0,1},{1,0},{2,3},{3,2},{4,5},{5,4},{6,7},{7,6},{8,9},{9,8},{10,11... | collective-permute-start | bytes 2359304 | tf_op jit(solution)/shard_map/ppermute | solution.py:325
  122.4 0.9 copy-start.2
  122.4 1.1 copy-start.3
  140.0 1.9 collective-permute-start.5
  142.0 0.8 copy-start.1
  168.8 1.7 copy-start
Sparse Core Ops, SparseCore 0:
  10.7 72.3 all-gather.2
  84.8 66.6 all-gather.4
